TPU v7x, 32 devices: a whole 2x2x4 slice. The times are simulated.
32 devices in a mesh: tm: 4 (over y, x), det: 8 (over z, core).
Axes of the slice: x: 2, y: 2, z: 4, core: 2. Of those that a mesh axis runs over, the one named last changes fastest.
Arguments:
- timestream: float32 [4, 128, 8192], P('tm', 'det'), may hold values from -0.8 to 0.8
- polar_angle: float32 [4, 128, 8192], P('tm', 'det'), may hold values from -3.140625 to 3.140625
- pixel_index: int32 [4, 128, 8192], P('tm', 'det'), may hold values from 0 to 2047
- strip_tile: int32 [4, 128, 64], P('tm', 'det'), may hold values from 0 to 7
- time_const: float32 [4, 128], P('tm', 'det'), may hold values from 0.2 to 2
- knee_freq: float32 [4, 128], P('tm', 'det'), may hold values from 0.005 to 0.05
- noise_slope: float32 [4, 128], P('tm', 'det'), may hold values from 1 to 3
- white_weight: float32 [4, 128], P('tm', 'det'), may hold values from 0.5 to 2
- mode_mix: float32 [4, 128, 64], P('tm', 'det'), may hold values from -1 to 1
- coupling: float32 [64, 64], replicated, may hold values from -1 to 2
- device_slots: int32 [4, 64], P('tm', 'det'), may hold values from 0 to 31, as said below
- slot_home: int32 [4, 32], P('tm', 'det'), may hold values from 0 to 31, as said below
Outputs:
- sky_map: float32 [256, 3, 2048], P(('tm', 'det'))
Inputs may be any that keep to these rules, and one draw needn't show every extreme that they name: `device_slots`: entries j * 8 to (j + 1) * 8 - 1 of a row are the entries of the group's tile list that device j of the group touches, all distinct. Of each block of 4 entries (those with the same entry // 4) a device touches exactly 2 in half of the blocks and exactly 0 in the others. `slot_home`: entry s of group g is owner_tm * 8 + place: the tile is held at place place by the device with tm index owner_tm and det index s // 4. Entries of one block of 4 are distinct; in every block exactly 2 entries share one owner_tm, and the others are spread as evenly as possible over the other owner_tm values.
All inputs are finite; a program needn't handle non-finite values.
Results may differ from a plain program's by a relative error of at most 0.0001.
Values sent between devices are 32-bit elements; how exact they have to be, the bound alone decides.
A program may use at most 64 MiB of HBM per device.

v0:
```python
import math

import jax
import jax.numpy as jnp
from jax import lax
from jax.sharding import PartitionSpec as P

SAMPLES = 4096
TILE_PIX = 2048
CAPD = 2
CAPT = 2
OWN = 8


HIGHEST = lax.Precision.HIGHEST


def fourier_table(length):
    counter = jnp.arange(length, dtype=jnp.int32)
    phases = counter[:, None] * counter[None, :] % length
    radians = 2.0 * math.pi / length * phases.astype(jnp.float32)
    return (jnp.cos(radians), jnp.sin(radians))


def twiddle_table(outer, inner, length):
    phases = (
        jnp.arange(outer, dtype=jnp.int32)[:, None]
        * jnp.arange(inner, dtype=jnp.int32)[None, :]
        % length
    )
    radians = 2.0 * math.pi / length * phases.astype(jnp.float32)
    return (jnp.cos(radians), jnp.sin(radians))


def forward_transform(signal):
    count, length = signal.shape
    outer = length // 128
    cos_outer, sin_outer = fourier_table(outer)
    cos_inner, sin_inner = fourier_table(128)
    cos_twist, sin_twist = twiddle_table(outer, 128, length)
    shaped = signal.reshape(count, outer, 128)
    first_real = jnp.einsum("rab,ak->rkb", shaped, cos_outer, precision=HIGHEST)
    first_imag = -jnp.einsum("rab,ak->rkb", shaped, sin_outer, precision=HIGHEST)
    twist_real = first_real * cos_twist + first_imag * sin_twist
    twist_imag = first_imag * cos_twist - first_real * sin_twist
    spec_real = jnp.einsum("rkb,bq->rkq", twist_real, cos_inner, precision=HIGHEST) + jnp.einsum(
        "rkb,bq->rkq", twist_imag, sin_inner, precision=HIGHEST
    )
    spec_imag = jnp.einsum("rkb,bq->rkq", twist_imag, cos_inner, precision=HIGHEST) - jnp.einsum(
        "rkb,bq->rkq", twist_real, sin_inner, precision=HIGHEST
    )
    return (spec_real, spec_imag)


def inverse_transform(spec_real, spec_imag):
    count, outer, inner = spec_real.shape
    length = outer * inner
    cos_outer, sin_outer = fourier_table(outer)
    cos_inner, sin_inner = fourier_table(inner)
    cos_twist, sin_twist = twiddle_table(outer, inner, length)
    section_real = jnp.einsum("rkq,qm->rkm", spec_real, cos_inner, precision=HIGHEST) - jnp.einsum(
        "rkq,qm->rkm", spec_imag, sin_inner, precision=HIGHEST
    )
    section_imag = jnp.einsum("rkq,qm->rkm", spec_imag, cos_inner, precision=HIGHEST) + jnp.einsum(
        "rkq,qm->rkm", spec_real, sin_inner, precision=HIGHEST
    )
    twist_real = section_real * cos_twist - section_imag * sin_twist
    twist_imag = section_imag * cos_twist + section_real * sin_twist
    result = jnp.einsum("rkm,kj->rjm", twist_real, cos_outer, precision=HIGHEST) - jnp.einsum(
        "rkm,kj->rjm", twist_imag, sin_outer, precision=HIGHEST
    )
    return result.reshape(count, length) / length


def bin_samples(stream, polar_angle, pixel_index, strip_slots, slot_total):
    det_count, total = stream.shape
    strips = strip_slots.shape[1]
    width = total // strips
    sample_slot = jnp.broadcast_to(strip_slots[:, :, None], (det_count, strips, width)).reshape(
        det_count, total
    )
    flat_index = (sample_slot * (3 * TILE_PIX) + pixel_index).reshape(-1)
    values = stream.reshape(-1)
    twice = 2.0 * polar_angle.reshape(-1)
    segment_ids = jnp.concatenate([flat_index, flat_index + TILE_PIX, flat_index + 2 * TILE_PIX])
    payload = jnp.concatenate([values, values * jnp.cos(twice), values * jnp.sin(twice)])
    sums = jax.ops.segment_sum(payload, segment_ids, num_segments=slot_total * 3 * TILE_PIX)
    return sums.reshape(slot_total, 3, TILE_PIX)


def pack_slots(items, target_peer, label, peers, capacity):
    count = target_peer.shape[0]
    counter = jnp.arange(count, dtype=jnp.int32)
    earlier = (target_peer[None, :] == target_peer[:, None]) & (counter[None, :] < counter[:, None])
    rank_in = jnp.sum(earlier.astype(jnp.int32), axis=1)
    target_slot = target_peer * capacity + rank_in
    slot_hits = target_slot[None, :] == jnp.arange(peers * capacity, dtype=jnp.int32)[:, None]
    source_row = jnp.sum(jnp.where(slot_hits, counter[None, :], 0), axis=1)
    filled = jnp.any(slot_hits, axis=1)
    payload = jnp.where(filled[:, None, None], items[source_row], 0.0)
    labels = jnp.where(filled, label[source_row], -1)
    return (payload.reshape(peers, capacity, 3, TILE_PIX), labels.reshape(peers, capacity))


def sum_received(payload, labels, slot_total):
    flat_rows = payload.reshape(-1, 3 * TILE_PIX)
    slot_hits = (
        labels.reshape(-1)[None, :] == jnp.arange(slot_total, dtype=jnp.int32)[:, None]
    ).astype(jnp.float32)
    summed = jnp.dot(slot_hits, flat_rows, precision=HIGHEST, preferred_element_type=jnp.float32)
    return summed.reshape(slot_total, 3, TILE_PIX)


def per_device(
    timestream,
    polar_angle,
    pixel_index,
    strip_tile,
    time_const,
    knee_freq,
    noise_slope,
    white_weight,
    mode_mix,
    coupling,
    device_slots,
    slot_home,
):
    det_count = timestream.shape[1]
    total = timestream.shape[2]
    length = SAMPLES
    scans = total // length
    outer = length // 128
    signal = timestream[0].reshape(det_count * scans, length)
    spec_real, spec_imag = forward_transform(signal)
    positions = jnp.arange(length, dtype=jnp.int32).reshape(128, outer).T
    frequency = ((positions + length // 2) % length - length // 2).astype(jnp.float32) / length
    slope_wide = noise_slope[0][:, None, None]
    power_law = jnp.power(jnp.abs(frequency)[None], slope_wide)
    weight = (
        white_weight[0][:, None, None]
        * power_law
        / (power_law + jnp.power(knee_freq[0][:, None, None], slope_wide))
    )
    lag_phase = 2.0 * math.pi * frequency[None] * time_const[0][:, None, None]
    spec_real = spec_real.reshape(det_count, scans, outer, 128)
    spec_imag = spec_imag.reshape(det_count, scans, outer, 128)
    weight_wide = weight[:, None]
    lag_wide = lag_phase[:, None]
    weighted_real = weight_wide * (spec_real - lag_wide * spec_imag)
    weighted_imag = weight_wide * (spec_imag + lag_wide * spec_real)
    stacked = jnp.stack([weighted_real, weighted_imag], axis=1).reshape(
        det_count, 2 * scans * length
    )
    mixing = mode_mix[0]
    amplitudes = jnp.dot(mixing.T, stacked, precision=HIGHEST, preferred_element_type=jnp.float32)
    summed = lax.psum(amplitudes, "det")
    coupled = jnp.dot(coupling, summed, precision=HIGHEST, preferred_element_type=jnp.float32)
    projected = jnp.dot(
        mixing, coupled, precision=HIGHEST, preferred_element_type=jnp.float32
    ).reshape(det_count, 2, scans, outer, 128)
    cleaned = stacked.reshape(det_count, 2, scans, outer, 128) - weight[:, None, None] * projected
    clean_real = cleaned[:, 0].reshape(det_count * scans, outer, 128)
    clean_imag = cleaned[:, 1].reshape(det_count * scans, outer, 128)
    stream = inverse_transform(clean_real, clean_imag).reshape(det_count, total)
    local_slots = device_slots[0]
    tile_count = local_slots.shape[0]
    gshare = slot_home.shape[1]
    partials = bin_samples(stream, polar_angle[0], pixel_index[0], strip_tile[0], tile_count)
    payload, labels = pack_slots(
        partials, local_slots // gshare, local_slots % gshare, lax.axis_size("det"), CAPD
    )
    got_payload, got_labels = (
        lax.all_to_all(payload, "det", split_axis=0, concat_axis=0, tiled=True),
        lax.all_to_all(labels, "det", split_axis=0, concat_axis=0, tiled=True),
    )
    block_sum = sum_received(got_payload, got_labels, gshare)
    home_code = slot_home[0]
    owner_payload, owner_labels = pack_slots(
        block_sum, home_code // OWN, home_code % OWN, lax.axis_size("tm"), CAPT
    )
    got_owner, got_places = (
        lax.all_to_all(owner_payload, "tm", split_axis=0, concat_axis=0, tiled=True),
        lax.all_to_all(owner_labels, "tm", split_axis=0, concat_axis=0, tiled=True),
    )
    return sum_received(got_owner, got_places, OWN)


def solution(mesh):
    placed = (
        P("tm", "det", None),
        P("tm", "det", None),
        P("tm", "det", None),
        P("tm", "det", None),
        P("tm", "det"),
        P("tm", "det"),
        P("tm", "det"),
        P("tm", "det"),
        P("tm", "det", None),
        P(),
        P("tm", "det"),
        P("tm", "det"),
    )
    return jax.shard_map(
        per_device,
        mesh=mesh,
        in_specs=placed,
        out_specs=P(("tm", "det"), None, None),
        check_vma=False,
    )
```

profile of v0, /device:TPU:0, one launch (start us, length us, event | category | flops | bytes accessed | tf_op | source)
XLA Modules:
  0.0 2240.6 jit_solution(6713187151320705484)
XLA Ops:
  6.6 1.1 reshape_reshape_squeeze.3
  7.8 0.7 convolution_negate_fusion
  8.4 0.7 fusion.64
  9.1 0.8 fusion.7
  9.9 0.8 fusion.3
  10.8 0.8 convolution_add_fusion.1
  11.7 0.8 convolution_subtract_fusion.2
  12.6 0.4 fusion.19
  13.0 0.2 subtract_multiply_fusion
  13.2 0.1 pad_maximum_fusion.1
  13.3 0.6 copy-done.3
  13.9 5.7 convolution_bitcast_fusion
  19.6 0.6 copy-done.9
  20.2 0.2 convert_reduce_fusion
  20.4 0.1 select_reduce_fusion
  20.5 0.1 fusion.83
  20.6 0.7 gather_fusion.1
  21.3 0.7 select_n.200
  22.0 6.3 all-to-all-start.1
  28.3 0.1 copy.45
  28.4 0.2 broadcast_in_dim.68
  28.8 1.3 pad_add_fusion
  30.1 0.1 broadcast_in_dim.65
  30.2 1.9 cosine_bitcast_fusion
  32.1 0.1 copy.48
  32.2 0.1 copy.49
  32.4 0.2 convert_reduce_fusion.1
  32.5 86.5 %all-reduce.2.cloned.1.call-done = f32[64,16384]{1,0:T(8,128)} async-done(((f32[64,16384]{1,0:T(8,128)}), f32[64,16384]{1,0:T(8,128)}) %all-reduce.2.cloned.1.call-update) | async-done | bytes 4194320 | tf_op jit(solution)/shard_map/psum | solution.py:156
  119.0 5.6 fusion.150
  124.7 2.3 convolution_bitcast_fusion.1
  126.9 0.2 copy.47
  127.1 0.3 multiply_subtract_fusion
  127.4 0.1 fusion.146
  127.5 0.8 fusion.35
  128.4 0.8 fusion.33
  129.2 0.8 convolution_subtract_fusion.1
  130.0 0.8 convolution_add_fusion
  130.8 0.7 fusion.12
  131.5 0.7 fusion
  132.2 0.1 fusion.147
  132.3 0.1 pad_maximum_fusion
  132.4 2065.7 %scatter_custom_fusion = f32[49152]{0:T(1024)S(1)} fusion(s32[393216]{0:T(1024)} %pad_add_fusion, f32[393216]{0:T(1024)S(1)} %pad_maximum_fusion, f32[]{:T(128)} %constant.130.clone.1), kind=kCustom, calls=%fused_computation.57 | custom fusion | flops 393216 | bytes 197120 | tf_op jit(solution)/shard_map/scatter-add | solution.py:87
  2198.2 0.9 gather_fusion.2
  2199.1 1.2 copy_select_fusion
  2200.3 3.6 all-to-all-start.2
  2203.8 0.1 fusion.89
  2203.9 0.1 broadcast_in_dim.60
  2204.1 0.6 gather_fusion
  2204.8 0.7 select_n.193
  2205.4 0.5 broadcast.601
  2206.0 0.6 reduce.6
  2206.6 9.8 all-to-all-done.2
  2216.4 3.2 all-to-all-start
  2219.6 0.3 copy.39
  2219.9 0.5 fusion.16
  2220.5 0.7 gather_fusion.3
  2221.2 0.9 copy_select_fusion.1
  2222.1 2.0 all-to-all-done
  2224.1 3.4 all-to-all-start.3
  2227.5 0.6 reduce.7
  2228.1 0.1 eq.114
  2228.2 4.5 all-to-all-done.3
  2232.6 0.1 copy.43
  2232.8 1.0 fusion.85
  (46 shorter events, 0.7 us)
Async XLA Ops:
  6.5 112.5 %copy-start = (f32[64,64]{1,0:T(8,128)S(1)}, f32[64,64]{1,0:T(8,128)}, u32[]{:S(2)}) copy-start(f32[64,64]{1,0:T(8,128)} %param.21) | copy-start | bytes 49156
  6.5 112.5 %all-reduce.2.cloned.1.call-start = ((), (), s32[]{:S(2)}) async-start(), calls=%async_computation.4 | async-start | bytes 8388608 | tf_op jit(solution)/shard_map/psum | solution.py:156
  11.6 0.9 copy-start.5
  11.6 0.9 copy-start.8
  11.6 0.9 copy-start.6
  11.7 0.9 copy-start.7
  13.2 0.7 copy-start.3
  19.6 0.7 copy-start.9
  19.6 8.7 copy-start.4
  19.6 8.8 copy-start.2
  22.0 2178.3 %all-to-all-start.1 = ((s32[8,1,2]{2,1,0:T(1,128)}), s32[8,1,2]{2,1,0:T(1,128)S(1)}, u32[]{:S(2)}, u32[]{:S(2)}) async-start(s32[8,1,2]{2,1,0:T(1,128)} %bitcast.14), calls=%async_computation.1 | async-start | bytes 8192 | tf_op jit(solution)/shard_map/all_to_all | solution.py:174
  28.8 1.4 copy-start.1
  30.2 2.1 copy-start.10
  2200.3 16.1 all-to-all-start.2
  2216.4 7.7 all-to-all-start
  2224.1 8.5 all-to-all-start.3
Sparse Core Ops, SparseCore 0:
  19.7 99.2 all-reduce.1
where the time goes:
time: 2240 us
  other arithmetic  2070 us (92%)
  waiting for transfers between devices  103 us (5%)
  matrix products  24.2 us (1%)
    scatter-add x1, other arithmetic, bin_samples(): jax.ops.segment_sum(payload, segment_ids, num_segments=slot_total * 3 * T...  2070 us
    psum x1, waiting for transfers between devices, per_device(): summed = lax.psum(amplitudes, 'det')  86.5 us
  transfers between devices with their start and end apart: 5, of which 4 were waited for; matrix products, arithmetic and copies ran while one was open for 93% of the time, Pallas kernels for 0%

commit v1 on v0

v1 whole, which is shorter than its diff:
```python
import functools
import math

import jax
import jax.numpy as jnp
import numpy as np
from jax import lax
from jax.experimental import pallas as pl
from jax.experimental.pallas import tpu as pltpu
from jax.sharding import PartitionSpec as P

SAMPLES = 4096
TILE_PIX = 2048
CAPD = 2
CAPT = 2
OWN = 8
LANES = 128
OUTER = SAMPLES // LANES
HALF = OUTER // 2
TILE_ROWS = 3 * TILE_PIX // LANES
PIX_ROWS = TILE_PIX // LANES
SLOT_ROWS = TILE_ROWS + 8

HIGHEST = lax.Precision.HIGHEST
VMEM_LIMIT = 56 * 1024 * 1024


def transform_tables():
    b = np.arange(LANES)[:, None]
    q = np.arange(LANES)[None, :]
    cos = np.cos(2 * np.pi * (b * q % LANES) / LANES)
    sin = np.sin(2 * np.pi * (b * q % LANES) / LANES)
    forward = np.block([[cos, -sin], [sin, cos]])
    backward = np.block([[cos, sin], [-sin, cos]]) / SAMPLES
    h = LANES // 2
    even_f = np.concatenate([cos[:, :h], -sin[:, :h]], axis=1)
    even_f[:, h] = cos[:, h]
    even_b = np.concatenate([2 * cos[:h], -2 * sin[:h]], axis=0)
    even_b[0] = 1.0
    even_b[h] = cos[h]
    odd_phase = 2 * np.pi * (b * (2 * np.arange(h)[None, :] + 1) % (2 * LANES)) / (2 * LANES)
    odd_f = np.concatenate([np.cos(odd_phase), -np.sin(odd_phase)], axis=1)
    odd_b = np.concatenate([2 * np.cos(odd_phase).T, -2 * np.sin(odd_phase).T], axis=0)
    zero = np.zeros((LANES, LANES))
    packed_f = np.block([[even_f, zero], [zero, odd_f]])
    packed_b = np.block([[even_b, zero], [zero, odd_b]]) / SAMPLES
    matrices = np.stack([packed_f, forward, packed_b, backward]).astype(np.float32)
    k1 = np.arange(HALF)[:, None]
    angle = 2 * np.pi * (k1 * q) / SAMPLES
    k = k1 + OUTER * q
    freq = (((k + SAMPLES // 2) % SAMPLES) - SAMPLES // 2) / SAMPLES
    lane = np.arange(LANES)
    low = lane % h
    even_k = OUTER * low
    even_k[h] = SAMPLES // 2
    odd_k = HALF + OUTER * low
    even_freq = (((even_k + SAMPLES // 2) % SAMPLES) - SAMPLES // 2) / SAMPLES
    odd_freq = (((odd_k + SAMPLES // 2) % SAMPLES) - SAMPLES // 2) / SAMPLES
    freq = np.concatenate([freq, odd_freq[None]], axis=0)
    freq[0] = even_freq
    with np.errstate(divide="ignore"):
        logs = np.where(freq == 0.0, -1e30, np.log2(np.abs(freq)))
    lag = 2 * np.pi * freq
    even_lag = np.where(lane < h, -lag[0], lag[0])
    even_lag[h] = 0.0
    even_lag[0] = 0.0
    odd_lag = np.where(lane < h, -lag[HALF], lag[HALF])
    lag[0] = even_lag
    lag[HALF] = odd_lag
    twist = np.stack([np.cos(angle), np.sin(angle)])
    rows = np.concatenate([twist[0], twist[1], logs, lag], axis=0)
    rows = np.concatenate([rows, np.zeros((-rows.shape[0] % 8, LANES))], axis=0)
    return matrices, rows.astype(np.float32)


ROW_COS, ROW_SIN, ROW_LOG, ROW_LAG = 0, HALF, 2 * HALF, 3 * HALF + 1


def add(x, y):
    return y if x is None else (x if y is None else x + y)


def sub(x, y):
    if y is None:
        return x
    return -y if x is None else x - y


def rotate(re, im, c, s):
    if abs(s) < 1e-12:
        return (re, im) if c > 0 else (-re, None if im is None else -im)
    if abs(c) < 1e-12:
        flip = None if im is None else (-im if s > 0 else im)
        return flip, (re if s > 0 else -re)
    if im is None:
        return re * c, re * s
    return re * c - im * s, im * c + re * s


def real_forward(xs):
    n = len(xs)
    if n == 1:
        return [xs[0]], [None]
    if n == 2:
        return [xs[0] + xs[1], xs[0] - xs[1]], [None, None]
    er, ei = real_forward(xs[0::2])
    odr, odi = real_forward(xs[1::2])
    re, im = [None] * (n // 2 + 1), [None] * (n // 2 + 1)
    for k in range(n // 4 + 1):
        angle = -2.0 * math.pi * k / n
        pr, pi_ = rotate(odr[k], odi[k], math.cos(angle), math.sin(angle))
        re[k], im[k] = add(er[k], pr), add(ei[k], pi_)
        if k < n // 4:
            re[n // 2 - k] = sub(er[k], pr)
            tail = sub(ei[k], pi_)
            im[n // 2 - k] = None if tail is None else -tail
    return re, im


def real_backward(re, im):
    n = 2 * (len(re) - 1)
    if n == 2:
        return [re[0] + re[1], re[0] - re[1]]
    er, ei, odr, odi = [], [], [], []
    for k in range(n // 4 + 1):
        m = n // 2 - k
        if k == 0:
            er.append(re[0] + re[m])
            ei.append(None)
            odr.append(re[0] - re[m])
            odi.append(None)
        elif k == m:
            er.append(2.0 * re[k])
            ei.append(None)
            odr.append(-2.0 * im[k])
            odi.append(None)
        else:
            er.append(re[k] + re[m])
            ei.append(im[k] - im[m])
            angle = 2.0 * math.pi * k / n
            pr, pi_ = rotate(re[k] - re[m], im[k] + im[m], math.cos(angle), math.sin(angle))
            odr.append(pr)
            odi.append(pi_)
    even, odd = real_backward(er, ei), real_backward(odr, odi)
    return [v for pair in zip(even, odd) for v in pair]


def split_bf16(x):
    high = x.astype(jnp.bfloat16)
    return high, (x - high.astype(jnp.float32)).astype(jnp.bfloat16)


def dot32(x, y):
    return jnp.dot(x, y, precision=HIGHEST, preferred_element_type=jnp.float32)


def column(row_ref, dets):
    wide = jnp.broadcast_to(row_ref[...], (dets, dets))
    own = lax.broadcasted_iota(jnp.int32, (dets, dets), 0) == lax.broadcasted_iota(jnp.int32, (dets, dets), 1)
    return jnp.sum(jnp.where(own, wide, 0.0), axis=1, keepdims=True)


def table_row(rows_ref, row, shape):
    return jnp.broadcast_to(rows_ref[row : row + 1, :], shape)


def spectra(ts_ref, tc_ref, knee_ref, slope_ref, white_ref, mat_ref, rows_ref, work_ref, w_ref, nw_ref):
    dets = ts_ref.shape[1]
    scans = ts_ref.shape[2] // SAMPLES
    for scan in range(scans):
        for d0 in range(0, dets, 8):
            xs = [ts_ref[0, d0 : d0 + 8, (scan * OUTER + a) * LANES : (scan * OUTER + a + 1) * LANES] for a in range(OUTER)]
            re, im = real_forward(xs)
            for k1 in range(HALF):
                r = (k1 * scans + scan) * dets + d0
                if k1 == 0:
                    out_re, out_im = re[0], re[HALF]
                else:
                    c = table_row(rows_ref, ROW_COS + k1, (8, LANES))
                    s = table_row(rows_ref, ROW_SIN + k1, (8, LANES))
                    out_re, out_im = re[k1] * c + im[k1] * s, im[k1] * c - re[k1] * s
                work_ref[r : r + 8, :LANES] = out_re
                work_ref[r : r + 8, LANES:] = out_im
    head = scans * dets
    work_ref[:head, :] = dot32(work_ref[:head, :], mat_ref[0])
    work_ref[head:, :] = dot32(work_ref[head:, :], mat_ref[1])
    slope, knee, tau = column(slope_ref, dets), column(knee_ref, dets), column(tc_ref, dets)
    white = column(white_ref, dets)
    knee_pow = jnp.exp2(slope * jnp.log2(knee))
    shape = (dets, LANES)
    slope, knee_pow = jnp.broadcast_to(slope, shape), jnp.broadcast_to(knee_pow, shape)
    tau, white = jnp.broadcast_to(tau, shape), jnp.broadcast_to(white, shape)
    for row in range(HALF + 1):
        power = jnp.exp2(slope * table_row(rows_ref, ROW_LOG + row, shape))
        weight = white * power / (power + knee_pow)
        nw_ref[row] = weight
        lag = tau * table_row(rows_ref, ROW_LAG + row, shape)
        for scan in range(scans):
            if row == 0 or row == HALF:
                r = scan * dets
                part = 0 if row == 0 else 1
                v = work_ref[r : r + dets, part * LANES : (part + 1) * LANES]
                w_ref[part * HALF * scans + scan] = weight * (v + lag * pltpu.roll(v, LANES // 2, 1))
            else:
                r = (row * scans + scan) * dets
                re, im = work_ref[r : r + dets, :LANES], work_ref[r : r + dets, LANES:]
                w_ref[row * scans + scan] = weight * (re - lag * im)
                w_ref[(HALF + row) * scans + scan] = weight * (im + lag * re)


def streams(w_ref, p_ref, nw_ref, mat_ref, rows_ref, work_ref, store):
    dets = w_ref.shape[1]
    scans = w_ref.shape[0] // (2 * HALF)
    for part in range(2):
        for k1 in range(HALF):
            row = HALF if (part == 1 and k1 == 0) else k1
            for scan in range(scans):
                i = (part * HALF + k1) * scans + scan
                r = (k1 * scans + scan) * dets
                work_ref[r : r + dets, part * LANES : (part + 1) * LANES] = w_ref[i] - nw_ref[row] * p_ref[i]
    head = scans * dets
    work_ref[:head, :] = dot32(work_ref[:head, :], mat_ref[2])
    work_ref[head:, :] = dot32(work_ref[head:, :], mat_ref[3])
    for scan in range(scans):
        for d0 in range(0, dets, 8):
            re, im = [], []
            for k1 in range(HALF):
                r = (k1 * scans + scan) * dets + d0
                zr, zi = work_ref[r : r + 8, :LANES], work_ref[r : r + 8, LANES:]
                if k1 == 0:
                    re.append(zr)
                    im.append(None)
                    last = zi
                else:
                    c = table_row(rows_ref, ROW_COS + k1, (8, LANES))
                    s = table_row(rows_ref, ROW_SIN + k1, (8, LANES))
                    re.append(zr * c - zi * s)
                    im.append(zi * c + zr * s)
            re.append(last)
            im.append(None)
            for a, value in enumerate(real_backward(re, im)):
                store(scan, d0, a, value)


def forward_kernel(n_det, ts_ref, tc_ref, knee_ref, slope_ref, white_ref, mix_ref, mat_ref, rows_ref,
                   send_ref, w_ref, nw_ref, work_ref):
    spectra(ts_ref, tc_ref, knee_ref, slope_ref, white_ref, mat_ref, rows_ref, work_ref, w_ref, nw_ref)
    share = w_ref.shape[0] // n_det
    modes = mix_ref.shape[2]
    for j in range(n_det):
        for r in range(share):
            send_ref[j, r] = w_ref[j * share + r]
        send_ref[j, share, :, :modes] = mix_ref[0]
        send_ref[j, share, :, modes:] = jnp.zeros((mix_ref.shape[1], LANES - modes), jnp.float32)


def couple_kernel(n_det, got_ref, cpl_ref, out_ref):
    share = got_ref.shape[1] - 1
    dets = got_ref.shape[2]
    modes = cpl_ref.shape[0]
    mix = jnp.concatenate([got_ref[j, share] for j in range(n_det)], axis=0)[:, :modes]
    shift = dot32(mix, cpl_ref[...])
    gram = lax.dot_general(shift, mix, (((1,), (1,)), ((), ())), precision=HIGHEST,
                           preferred_element_type=jnp.float32)
    for r in range(share):
        block = jnp.concatenate([got_ref[j, r] for j in range(n_det)], axis=0)
        back = dot32(gram, block)
        for j in range(n_det):
            out_ref[j, r] = back[j * dets : (j + 1) * dets]


def backward_kernel(w_ref, p_ref, nw_ref, mat_ref, rows_ref, out_ref, work_ref):
    def store(scan, d0, a, value):
        s = scan * OUTER + a
        out_ref[s, d0 : d0 + 8, :] = value

    streams(w_ref, p_ref, nw_ref, mat_ref, rows_ref, work_ref, store)


def turn_polynomials():
    x = (np.cos(np.pi * (np.arange(400) + 0.5) / 400) + 1) / 8
    t = np.sqrt(x)
    cheb = np.polynomial.Polynomial
    cos_fit = cheb.fit(x, np.cos(2 * np.pi * t), 7).convert().coef
    sin_fit = cheb.fit(x, np.sin(2 * np.pi * t) / t, 7).convert().coef
    return [float(np.float32(c)) for c in cos_fit], [float(np.float32(c)) for c in sin_fit]


COS_FIT, SIN_FIT = turn_polynomials()


def horner(coefficients, x):
    total = jnp.full_like(x, coefficients[-1])
    for c in coefficients[-2::-1]:
        total = total * x + c
    return total


def bin_kernel(gshare, stream_ref, angle_ref, pix_ref, tile_ref, slots_ref, out_ref, target_ref, count_ref):
    strips, dets, _ = stream_ref.shape
    n_slots = slots_ref.shape[1]
    peers = out_ref.shape[0] // CAPD

    def clear(i, carry):
        out_ref[i, :TILE_ROWS, :] = jnp.zeros((TILE_ROWS, LANES), jnp.float32)
        out_ref[i, TILE_ROWS:, :] = jnp.full((8, LANES), -1.0, jnp.float32)
        return carry

    lax.fori_loop(0, peers * CAPD, clear, 0)

    def reset(i, carry):
        count_ref[i] = 0
        return carry

    lax.fori_loop(0, peers, reset, 0)

    def place(i, carry):
        entry = slots_ref[0, i]
        peer = entry // gshare
        rank = count_ref[peer]
        count_ref[peer] = rank + 1
        target = peer * CAPD + rank
        target_ref[i] = target
        out_ref[target, TILE_ROWS:, :] = jnp.full((8, LANES), (entry - peer * gshare).astype(jnp.float32))
        return carry

    lax.fori_loop(0, n_slots, place, 0)

    low_iota = lax.broadcasted_iota(jnp.int32, (LANES, LANES), 0).astype(jnp.float32).astype(jnp.bfloat16)
    high_iota = lax.broadcasted_iota(jnp.int32, (PIX_ROWS, LANES), 0).astype(jnp.float32).astype(jnp.bfloat16)
    one, zero = jnp.bfloat16(1.0), jnp.bfloat16(0.0)

    def strip(s, carry):
        lanes = pl.ds(pl.multiple_of(s * LANES, LANES), LANES)
        value = stream_ref[s]
        turn = angle_ref[0, :, lanes] * (1.0 / math.pi)
        turn = turn - jnp.round(turn)
        square = turn * turn
        parts = [value, value * horner(COS_FIT, square), value * turn * horner(SIN_FIT, square)]
        halves = [split_bf16(v) for v in parts]
        halves = [h[0] for h in halves] + [h[1] for h in halves]
        pix = pix_ref[0, :, lanes]
        high = (pix >> 7).astype(jnp.float32).astype(jnp.bfloat16)
        low = (pix & (LANES - 1)).astype(jnp.float32).astype(jnp.bfloat16)
        for d in range(dets):
            hit = high_iota == high[d : d + 1, :]
            rows = jnp.concatenate([jnp.where(hit, h[d : d + 1, :], zero) for h in halves], axis=0)
            spread = jnp.where(low_iota == low[d : d + 1, :], one, zero)
            both = lax.dot_general(rows, spread, (((1,), (1,)), ((), ())), preferred_element_type=jnp.float32)
            target = target_ref[tile_ref[0, d, s]]
            out_ref[target, :TILE_ROWS, :] += both[:TILE_ROWS] + both[TILE_ROWS:]
        return carry

    lax.fori_loop(0, strips, strip, 0)


def regroup_kernel(got_ref, home_ref, out_ref, block_ref, count_ref):
    gshare = home_ref.shape[1]
    received = got_ref.shape[0]
    peers = out_ref.shape[0] // CAPT
    block_ref[...] = jnp.zeros_like(block_ref)

    def gather(i, carry):
        label = got_ref[i, TILE_ROWS : TILE_ROWS + 1, :]
        tile = got_ref[i, :TILE_ROWS, :]
        for e in range(gshare):
            block_ref[e] += jnp.where(label == float(e), tile, 0.0)
        return carry

    lax.fori_loop(0, received, gather, 0)
    out_ref[:, :TILE_ROWS, :] = jnp.zeros((peers * CAPT, TILE_ROWS, LANES), jnp.float32)
    out_ref[:, TILE_ROWS:, :] = jnp.full((peers * CAPT, 8, LANES), -1.0, jnp.float32)
    for p in range(peers):
        count_ref[p] = 0
    for e in range(gshare):
        code = home_ref[0, e]
        peer = code // OWN
        rank = count_ref[peer]
        count_ref[peer] = rank + 1
        target = peer * CAPT + rank
        out_ref[target, :TILE_ROWS, :] = block_ref[e]
        out_ref[target, TILE_ROWS:, :] = jnp.full((8, LANES), (code - peer * OWN).astype(jnp.float32))


def final_kernel(got_ref, out_ref):
    for t in range(OWN):
        for c in range(3):
            total = jnp.zeros((PIX_ROWS, LANES), jnp.float32)
            for i in range(got_ref.shape[0]):
                label = got_ref[i, TILE_ROWS : TILE_ROWS + 1, :]
                total = total + jnp.where(label == float(t), got_ref[i, c * PIX_ROWS : (c + 1) * PIX_ROWS, :], 0.0)
            out_ref[t, c] = total


def per_device(timestream, polar_angle, pixel_index, strip_tile, time_const, knee_freq, noise_slope,
               white_weight, mode_mix, coupling, device_slots, slot_home):
    dets, total = timestream.shape[1:]
    scans = total // SAMPLES
    n_det, n_tm = lax.axis_size("det"), lax.axis_size("tm")
    matrices, rows = transform_tables()
    matrices, rows = jnp.asarray(matrices), jnp.asarray(rows)
    blocks = 2 * HALF * scans
    share = blocks // n_det
    f32 = jnp.float32
    vmem = pl.BlockSpec(memory_space=pltpu.VMEM)
    smem = pl.BlockSpec(memory_space=pltpu.SMEM)
    params = pltpu.CompilerParams(vmem_limit_bytes=VMEM_LIMIT)
    work = pltpu.VMEM((HALF * scans * dets, 2 * LANES), f32)
    send, weighted, weight = pl.pallas_call(
        functools.partial(forward_kernel, n_det),
        out_shape=(
            jax.ShapeDtypeStruct((n_det, share + 1, dets, LANES), f32),
            jax.ShapeDtypeStruct((blocks, dets, LANES), f32),
            jax.ShapeDtypeStruct((HALF + 1, dets, LANES), f32),
        ),
        in_specs=[vmem] * 8,
        out_specs=(vmem,) * 3,
        scratch_shapes=[work],
        compiler_params=params,
        name="forward",
    )(timestream, time_const, knee_freq, noise_slope, white_weight, mode_mix, matrices, rows)
    got = lax.all_to_all(send, "det", split_axis=0, concat_axis=0, tiled=True)
    back = pl.pallas_call(
        functools.partial(couple_kernel, n_det),
        out_shape=jax.ShapeDtypeStruct((n_det, share, dets, LANES), f32),
        in_specs=[vmem] * 2,
        out_specs=vmem,
        compiler_params=params,
        name="couple",
    )(got, coupling)
    projected = lax.all_to_all(back, "det", split_axis=0, concat_axis=0, tiled=True).reshape(blocks, dets, LANES)
    stream = pl.pallas_call(
        backward_kernel,
        out_shape=jax.ShapeDtypeStruct((scans * OUTER, dets, LANES), f32),
        in_specs=[vmem] * 5,
        out_specs=vmem,
        scratch_shapes=[work],
        compiler_params=params,
        name="backward",
    )(weighted, projected, weight, matrices, rows)
    tiles = pl.pallas_call(
        functools.partial(bin_kernel, slot_home.shape[1]),
        out_shape=jax.ShapeDtypeStruct((n_det * CAPD, SLOT_ROWS, LANES), f32),
        in_specs=[vmem] * 3 + [smem] * 2,
        out_specs=vmem,
        scratch_shapes=[pltpu.SMEM((device_slots.shape[1],), jnp.int32), pltpu.SMEM((n_det,), jnp.int32)],
        compiler_params=params,
        name="binning",
    )(stream, polar_angle, pixel_index, strip_tile, device_slots)
    tiles = lax.all_to_all(tiles, "det", split_axis=0, concat_axis=0, tiled=True)
    homes = pl.pallas_call(
        regroup_kernel,
        out_shape=jax.ShapeDtypeStruct((n_tm * CAPT, SLOT_ROWS, LANES), f32),
        in_specs=[vmem, smem],
        out_specs=vmem,
        scratch_shapes=[pltpu.VMEM((slot_home.shape[1], TILE_ROWS, LANES), f32), pltpu.SMEM((n_tm,), jnp.int32)],
        compiler_params=params,
        name="regroup",
    )(tiles, slot_home)
    homes = lax.all_to_all(homes, "tm", split_axis=0, concat_axis=0, tiled=True)
    out = pl.pallas_call(
        final_kernel,
        out_shape=jax.ShapeDtypeStruct((OWN, 3, PIX_ROWS, LANES), f32),
        in_specs=[vmem],
        out_specs=vmem,
        compiler_params=params,
        name="place",
    )(homes)
    return out.reshape(OWN, 3, TILE_PIX)


def solution(mesh):
    placed = (
        P("tm", "det", None),
        P("tm", "det", None),
        P("tm", "det", None),
        P("tm", "det", None),
        P("tm", "det"),
        P("tm", "det"),
        P("tm", "det"),
        P("tm", "det"),
        P("tm", "det", None),
        P(),
        P("tm", "det"),
        P("tm", "det"),
    )
    return jax.shard_map(
        per_device,
        mesh=mesh,
        in_specs=placed,
        out_specs=P(("tm", "det"), None, None),
        check_vma=False,
    )
```

time: 2240 us -> 120 us (0.05)
  other arithmetic: 2070 us -> 0 us
  waiting for transfers between devices: 103 us -> 0 us
  blocking collectives: 0 us -> 70.4 us
  Pallas kernels: 0 us -> 47 us
  matrix products: 24.2 us -> 0 us
    scatter-add x1 -> x0, other arithmetic: 2070 us -> none  [bin_samples(): jax.ops.segment_sum(payload, segment_ids, num_segments=slot_total * 3 * T...]
    psum x1 -> x0, waiting for transfers between devices: 86.5 us -> none  [per_device(): summed = lax.psum(amplitudes, 'det')]
    all_to_all x0 -> x4, blocking collectives: none -> 70.4 us  [the longest x1 23.2 us: per_device(): got = lax.all_to_all(send, 'det', split_axis=0, concat_axis=0, tiled=True)]
    pallas_call x0 -> x6, Pallas kernels: none -> 47 us  [the longest x1 33.7 us: per_device(): pl.pallas_call(functools.partial(bin_kernel, slot_home.shape[1]), out_sha...]
    dot_general x17 -> x0, matrix products: 24.2 us -> none  [the longest x1 5.67 us: per_device(): jnp.dot(mixing.T, stacked, precision=HIGHEST, preferred_element_type=jnp....]
  transfers between devices with their start and end apart: 5 -> 0, of which waited for: 4 -> 0; matrix products, arithmetic and copies ran while one was open for 93% -> 0% of each run, Pallas kernels for 0% -> 0%
where the time goes in v1:
time: 120 us; the launch traced here: 119 us
  blocking collectives  70.4 us (59%)
  Pallas kernels  47 us (39%)
  local copies, waits for them, and re-layouts  1.65 us (1%)
    pallas_call x1, Pallas kernels, per_device(): pl.pallas_call(functools.partial(bin_kernel, slot_home.shape[1]), out_sha...  33.7 us
    all_to_all x1, blocking collectives, per_device(): got = lax.all_to_all(send, 'det', split_axis=0, concat_axis=0, tiled=True)  23.2 us
    all_to_all x1, blocking collectives, per_device(): lax.all_to_all(back, 'det', split_axis=0, concat_axis=0, tiled=True)  19.5 us
    all_to_all x1, blocking collectives, per_device(): lax.all_to_all(tiles, 'det', split_axis=0, concat_axis=0, tiled=True)  18.1 us
    all_to_all x1, blocking collectives, per_device(): homes = lax.all_to_all(homes, 'tm', split_axis=0, concat_axis=0, tiled=True)  9.71 us
    pallas_call x1, Pallas kernels, per_device(): pl.pallas_call(functools.partial(forward_kernel, n_det), out_shape=(jax.S...  3.35 us
    pallas_call x1, Pallas kernels, per_device(): pl.pallas_call(backward_kernel, out_shape=jax.ShapeDtypeStruct((scans * O...  3.18 us
    pallas_call x1, Pallas kernels, per_device(): pl.pallas_call(functools.partial(couple_kernel, n_det), out_shape=jax.Sha...  2.99 us

profile of v1, /device:TPU:0, one launch (start us, length us, event | category | flops | bytes accessed | tf_op | source)
XLA Modules:
  0.0 119.1 jit_solution(11596780215751451545)
XLA Ops:
  0.0 3.4 %forward.1 = (f32[8,9,16,128]{3,2,1,0:T(8,128)}, f32[64,16,128]{2,1,0:T(8,128)}, f32[17,16,128]{2,1,0:T(8,128)}) custom-call(f32[1,16,8192]{2,1,0:T(8,128)} %ts_ref.1, f32[1,16]{1,0:T(1,128)} %tc_ref.1, f32[1,16]{1,0:T(1,128)} %knee_ref.1, f32[1,16]{1,0:T(1,128)} %slope_ref.1, f32[1,16]{1,0:T(1,128)} %white_ref.1, f32[1,16,64]{2,1,0:T(8,128)} %mix_ref.1, ...), custom_call_target="tpu_custom_call" | custom-call | tf_op jit(solution)/shard_map/forward/pallas_call | solution.py:409
  3.4 23.2 %all_to_all.20.got_ref = f32[8,9,16,128]{3,2,1,0:T(8,128)} all-to-all(f32[8,9,16,128]{3,2,1,0:T(8,128)} %get-tuple-element.9), channel_id=1, replica_groups=mesh['tm'=4,'det'=8] {'det'}, dimensions={0} | all-to-all | bytes 1179648 | tf_op jit(solution)/shard_map/all_to_all | solution.py:422
  26.5 3.0 %couple.1 = f32[8,8,16,128]{3,2,1,0:T(8,128)} custom-call(f32[8,9,16,128]{3,2,1,0:T(8,128)} %all_to_all.20.got_ref, f32[64,64]{1,0:T(8,128)} %cpl_ref.1), custom_call_target="tpu_custom_call" | custom-call | tf_op jit(solution)/shard_map/couple/pallas_call | solution.py:423
  29.5 19.5 %all_to_all.21 = f32[8,8,16,128]{3,2,1,0:T(8,128)} all-to-all(f32[8,8,16,128]{3,2,1,0:T(8,128)} %couple.1), channel_id=1, replica_groups=mesh['tm'=4,'det'=8] {'det'}, dimensions={0} | all-to-all | bytes 1048576 | tf_op jit(solution)/shard_map/all_to_all | solution.py:431
  49.0 3.2 %backward.1.stream_ref = f32[64,16,128]{2,1,0:T(8,128)} custom-call(f32[64,16,128]{2,1,0:T(8,128)} %get-tuple-element.8.w_ref, f32[64,16,128]{2,1,0:T(8,128)} %bitcast.5, f32[17,16,128]{2,1,0:T(8,128)} %get-tuple-element.10.nw_ref, f32[4,256,256]{2,1,0:T(8,128)} %constant.4.clone.mat_ref, f32[72,128]{1,0:T(8,128)} %constant.5.clone.rows_ref), custom_call_target="tpu_custom_call" | custom-call | tf_op jit(solution)/shard_map/backward/pallas_call | solution.py:432
  52.2 33.7 %binning.1 = f32[16,56,128]{2,1,0:T(8,128)} custom-call(f32[64,16,128]{2,1,0:T(8,128)} %backward.1.stream_ref, f32[1,16,8192]{2,1,0:T(8,128)} %angle_ref.1, s32[1,16,8192]{2,1,0:T(8,128)} %pix_ref.1, s32[1,16,64]{2,1,0:T(8,128)} %tile_ref.1, s32[1,8]{1,0:T(1,128)} %slots_ref.1), custom_call_target="tpu_custom_call" | custom-call | tf_op jit(solution)/shard_map/binning/pallas_call | solution.py:441
  85.9 18.1 %all_to_all.22.got_ref = f32[16,56,128]{2,1,0:T(8,128)} all-to-all(f32[16,56,128]{2,1,0:T(8,128)} %binning.1), channel_id=1, replica_groups=mesh['tm'=4,'det'=8] {'det'}, dimensions={0} | all-to-all | bytes 917504 | tf_op jit(solution)/shard_map/all_to_all | solution.py:450
  104.0 2.0 %regroup.1 = f32[8,56,128]{2,1,0:T(8,128)} custom-call(f32[16,56,128]{2,1,0:T(8,128)} %all_to_all.22.got_ref, s32[1,4]{1,0:T(1,128)} %home_ref.1), custom_call_target="tpu_custom_call" | custom-call | tf_op jit(solution)/shard_map/regroup/pallas_call | solution.py:451
  106.0 9.7 %all_to_all.23.got_ref = f32[8,56,128]{2,1,0:T(8,128)} all-to-all(f32[8,56,128]{2,1,0:T(8,128)} %regroup.1), channel_id=1, replica_groups=mesh['tm'=4,'det'=8] {'tm'}, dimensions={0} | all-to-all | bytes 458752 | tf_op jit(solution)/shard_map/all_to_all | solution.py:460
  115.7 1.7 %place.1 = f32[8,3,16,128]{3,2,1,0:T(8,128)} custom-call(f32[8,56,128]{2,1,0:T(8,128)} %all_to_all.23.got_ref), custom_call_target="tpu_custom_call" | custom-call | tf_op jit(solution)/shard_map/place/pallas_call | solution.py:461
  117.4 0.9 copy.16
  118.4 0.7 reshape.7

commit v2 on v1

v2 whole, which is shorter than its diff:
```python
import functools
import math

import jax
import jax.numpy as jnp
import numpy as np
from jax import lax
from jax.experimental import pallas as pl
from jax.experimental.pallas import tpu as pltpu
from jax.sharding import PartitionSpec as P

SAMPLES = 4096
TILE_PIX = 2048
CAPD = 2
CAPT = 2
OWN = 8
LANES = 128
OUTER = SAMPLES // LANES
HALF = OUTER // 2
TILE_ROWS = 3 * TILE_PIX // LANES
PIX_ROWS = TILE_PIX // LANES
SLOT_ROWS = TILE_ROWS + 8

HIGHEST = lax.Precision.HIGHEST
VMEM_LIMIT = 56 * 1024 * 1024


def transform_tables():
    b = np.arange(LANES)[:, None]
    q = np.arange(LANES)[None, :]
    cos = np.cos(2 * np.pi * (b * q % LANES) / LANES)
    sin = np.sin(2 * np.pi * (b * q % LANES) / LANES)
    forward = np.block([[cos, -sin], [sin, cos]])
    backward = np.block([[cos, sin], [-sin, cos]]) / SAMPLES
    h = LANES // 2
    even_f = np.concatenate([cos[:, :h], -sin[:, :h]], axis=1)
    even_f[:, h] = cos[:, h]
    even_b = np.concatenate([2 * cos[:h], -2 * sin[:h]], axis=0)
    even_b[0] = 1.0
    even_b[h] = cos[h]
    odd_phase = 2 * np.pi * (b * (2 * np.arange(h)[None, :] + 1) % (2 * LANES)) / (2 * LANES)
    odd_f = np.concatenate([np.cos(odd_phase), -np.sin(odd_phase)], axis=1)
    odd_b = np.concatenate([2 * np.cos(odd_phase).T, -2 * np.sin(odd_phase).T], axis=0)
    zero = np.zeros((LANES, LANES))
    packed_f = np.block([[even_f, zero], [zero, odd_f]])
    packed_b = np.block([[even_b, zero], [zero, odd_b]]) / SAMPLES
    matrices = np.stack([packed_f, forward, packed_b, backward]).astype(np.float32)
    k1 = np.arange(HALF)[:, None]
    angle = 2 * np.pi * (k1 * q) / SAMPLES
    k = k1 + OUTER * q
    freq = (((k + SAMPLES // 2) % SAMPLES) - SAMPLES // 2) / SAMPLES
    lane = np.arange(LANES)
    low = lane % h
    even_k = OUTER * low
    even_k[h] = SAMPLES // 2
    odd_k = HALF + OUTER * low
    even_freq = (((even_k + SAMPLES // 2) % SAMPLES) - SAMPLES // 2) / SAMPLES
    odd_freq = (((odd_k + SAMPLES // 2) % SAMPLES) - SAMPLES // 2) / SAMPLES
    freq = np.concatenate([freq, odd_freq[None]], axis=0)
    freq[0] = even_freq
    with np.errstate(divide="ignore"):
        logs = np.where(freq == 0.0, -1e30, np.log2(np.abs(freq)))
    lag = 2 * np.pi * freq
    even_lag = np.where(lane < h, -lag[0], lag[0])
    even_lag[h] = 0.0
    even_lag[0] = 0.0
    odd_lag = np.where(lane < h, -lag[HALF], lag[HALF])
    lag[0] = even_lag
    lag[HALF] = odd_lag
    twist = np.stack([np.cos(angle), np.sin(angle)])
    rows = np.concatenate([twist[0], twist[1], logs, lag], axis=0)
    rows = np.concatenate([rows, np.zeros((-rows.shape[0] % 8, LANES))], axis=0)
    return matrices, rows.astype(np.float32)


ROW_COS, ROW_SIN, ROW_LOG, ROW_LAG = 0, HALF, 2 * HALF, 3 * HALF + 1


def add(x, y):
    return y if x is None else (x if y is None else x + y)


def sub(x, y):
    if y is None:
        return x
    return -y if x is None else x - y


def rotate(re, im, c, s):
    if abs(s) < 1e-12:
        return (re, im) if c > 0 else (-re, None if im is None else -im)
    if abs(c) < 1e-12:
        flip = None if im is None else (-im if s > 0 else im)
        return flip, (re if s > 0 else -re)
    if im is None:
        return re * c, re * s
    return re * c - im * s, im * c + re * s


def real_forward(xs):
    n = len(xs)
    if n == 1:
        return [xs[0]], [None]
    if n == 2:
        return [xs[0] + xs[1], xs[0] - xs[1]], [None, None]
    er, ei = real_forward(xs[0::2])
    odr, odi = real_forward(xs[1::2])
    re, im = [None] * (n // 2 + 1), [None] * (n // 2 + 1)
    for k in range(n // 4 + 1):
        angle = -2.0 * math.pi * k / n
        pr, pi_ = rotate(odr[k], odi[k], math.cos(angle), math.sin(angle))
        re[k], im[k] = add(er[k], pr), add(ei[k], pi_)
        if k < n // 4:
            re[n // 2 - k] = sub(er[k], pr)
            tail = sub(ei[k], pi_)
            im[n // 2 - k] = None if tail is None else -tail
    return re, im


def real_backward(re, im):
    n = 2 * (len(re) - 1)
    if n == 2:
        return [re[0] + re[1], re[0] - re[1]]
    er, ei, odr, odi = [], [], [], []
    for k in range(n // 4 + 1):
        m = n // 2 - k
        if k == 0:
            er.append(re[0] + re[m])
            ei.append(None)
            odr.append(re[0] - re[m])
            odi.append(None)
        elif k == m:
            er.append(2.0 * re[k])
            ei.append(None)
            odr.append(-2.0 * im[k])
            odi.append(None)
        else:
            er.append(re[k] + re[m])
            ei.append(im[k] - im[m])
            angle = 2.0 * math.pi * k / n
            pr, pi_ = rotate(re[k] - re[m], im[k] + im[m], math.cos(angle), math.sin(angle))
            odr.append(pr)
            odi.append(pi_)
    even, odd = real_backward(er, ei), real_backward(odr, odi)
    return [v for pair in zip(even, odd) for v in pair]


def split_bf16(x):
    high = x.astype(jnp.bfloat16)
    return high, (x - high.astype(jnp.float32)).astype(jnp.bfloat16)


def dot32(x, y):
    return jnp.dot(x, y, precision=HIGHEST, preferred_element_type=jnp.float32)


def column(row_ref, dets):
    wide = jnp.broadcast_to(row_ref[...], (dets, dets))
    own = lax.broadcasted_iota(jnp.int32, (dets, dets), 0) == lax.broadcasted_iota(jnp.int32, (dets, dets), 1)
    return jnp.sum(jnp.where(own, wide, 0.0), axis=1, keepdims=True)


def table_row(rows_ref, row, shape):
    return jnp.broadcast_to(rows_ref[row : row + 1, :], shape)


def noise_weights(tc_ref, knee_ref, slope_ref, white_ref, rows_ref, nw_ref, lag_ref):
    dets = tc_ref.shape[1]
    shape = (dets, LANES)
    slope, knee = column(slope_ref, dets), column(knee_ref, dets)
    knee_pow = jnp.broadcast_to(jnp.exp2(slope * jnp.log2(knee)), shape)
    slope = jnp.broadcast_to(slope, shape)
    tau, white = jnp.broadcast_to(column(tc_ref, dets), shape), jnp.broadcast_to(column(white_ref, dets), shape)
    for row in range(HALF + 1):
        power = jnp.exp2(slope * table_row(rows_ref, ROW_LOG + row, shape))
        nw_ref[row] = white * power / (power + knee_pow)
        lag_ref[row] = tau * table_row(rows_ref, ROW_LAG + row, shape)


def spectra(scan, ts_ref, mat_ref, rows_ref, nw_ref, lag_ref, work_ref, w_ref):
    dets = ts_ref.shape[1]
    for d0 in range(0, dets, 8):
        xs = [ts_ref[0, d0 : d0 + 8, (scan * OUTER + a) * LANES : (scan * OUTER + a + 1) * LANES] for a in range(OUTER)]
        re, im = real_forward(xs)
        for k1 in range(HALF):
            r = k1 * dets + d0
            if k1 == 0:
                out_re, out_im = re[0], re[HALF]
            else:
                c = table_row(rows_ref, ROW_COS + k1, (8, LANES))
                s = table_row(rows_ref, ROW_SIN + k1, (8, LANES))
                out_re, out_im = re[k1] * c + im[k1] * s, im[k1] * c - re[k1] * s
            work_ref[r : r + 8, :LANES] = out_re
            work_ref[r : r + 8, LANES:] = out_im
    work_ref[:dets, :] = dot32(work_ref[:dets, :], mat_ref[0])
    work_ref[dets:, :] = dot32(work_ref[dets:, :], mat_ref[1])
    for k1 in range(HALF):
        r = k1 * dets
        re, im = work_ref[r : r + dets, :LANES], work_ref[r : r + dets, LANES:]
        if k1 == 0:
            w_ref[scan, 0] = nw_ref[0] * (re + lag_ref[0] * pltpu.roll(re, LANES // 2, 1))
            w_ref[scan, HALF] = nw_ref[HALF] * (im + lag_ref[HALF] * pltpu.roll(im, LANES // 2, 1))
        else:
            w_ref[scan, k1] = nw_ref[k1] * (re - lag_ref[k1] * im)
            w_ref[scan, HALF + k1] = nw_ref[k1] * (im + lag_ref[k1] * re)


def streams(scan, w_ref, p_ref, nw_ref, mat_ref, rows_ref, work_ref, out_ref):
    dets = w_ref.shape[2]
    for part in range(2):
        for k1 in range(HALF):
            row = HALF if (part == 1 and k1 == 0) else k1
            i = part * HALF + k1
            r = k1 * dets
            work_ref[r : r + dets, part * LANES : (part + 1) * LANES] = w_ref[scan, i] - nw_ref[row] * p_ref[scan, i]
    work_ref[:dets, :] = dot32(work_ref[:dets, :], mat_ref[2])
    work_ref[dets:, :] = dot32(work_ref[dets:, :], mat_ref[3])
    for d0 in range(0, dets, 8):
        re, im = [], []
        for k1 in range(HALF):
            r = k1 * dets + d0
            zr, zi = work_ref[r : r + 8, :LANES], work_ref[r : r + 8, LANES:]
            if k1 == 0:
                re.append(zr)
                im.append(None)
                last = zi
            else:
                c = table_row(rows_ref, ROW_COS + k1, (8, LANES))
                s = table_row(rows_ref, ROW_SIN + k1, (8, LANES))
                re.append(zr * c - zi * s)
                im.append(zi * c + zr * s)
        re.append(last)
        im.append(None)
        for a, value in enumerate(real_backward(re, im)):
            out_ref[scan * OUTER + a, d0 : d0 + 8, :] = value


def remote(src, dst, send_sem, recv_sem, device):
    return pltpu.make_async_remote_copy(
        src_ref=src, dst_ref=dst, send_sem=send_sem, recv_sem=recv_sem, device_id=device,
        device_id_type=pl.DeviceIdType.MESH,
    )


def clean_kernel(n, ts_ref, tc_ref, knee_ref, slope_ref, white_ref, mix_ref, cpl_ref, mat_ref, rows_ref, out_ref,
                 w_ref, p_ref, nw_ref, lag_ref, work_ref, mine_ref, mix_all_ref, got_ref, back_ref,
                 mix_sems, out_sems, back_sems):
    me = lax.axis_index("det")
    scans, rows_all, dets, _ = w_ref.shape
    share = rows_all // n
    modes = mix_ref.shape[2]
    offsets = range(1, n)
    ahead = [lax.rem(me + o, n) for o in range(n)]
    behind = [lax.rem(me + n - o, n) for o in range(n)]
    barrier = pltpu.get_barrier_semaphore()
    for o in offsets:
        pl.semaphore_signal(barrier, inc=1, device_id={"det": ahead[o]}, device_id_type=pl.DeviceIdType.MESH)
    pl.semaphore_wait(barrier, n - 1)
    mine = jnp.concatenate([mix_ref[0], jnp.zeros((dets, LANES - modes), jnp.float32)], axis=1)
    mine_ref[...] = mine
    mix_all_ref[0] = mine
    copies = []
    for o in offsets:
        copy = remote(mine_ref, mix_all_ref.at[o], mix_sems.at[0, o], mix_sems.at[1, o], {"det": ahead[o]})
        copy.start()
        copies.append(copy)
    noise_weights(tc_ref, knee_ref, slope_ref, white_ref, rows_ref, nw_ref, lag_ref)
    outgoing = []
    for scan in range(scans):
        spectra(scan, ts_ref, mat_ref, rows_ref, nw_ref, lag_ref, work_ref, w_ref)
        sent = []
        for o in offsets:
            copy = remote(w_ref.at[scan, pl.ds(ahead[o] * share, share)], got_ref.at[scan, o],
                          out_sems.at[0, scan, o], out_sems.at[1, scan, o], {"det": ahead[o]})
            copy.start()
            sent.append(copy)
        outgoing.append(sent)
        got_ref[scan, 0] = w_ref[scan, pl.ds(me * share, share)]
    for copy in copies:
        copy.wait()
    mix = jnp.concatenate([mix_all_ref[o] for o in range(n)], axis=0)[:, :modes]
    gram = lax.dot_general(dot32(mix, cpl_ref[...]), mix, (((1,), (1,)), ((), ())), precision=HIGHEST,
                           preferred_element_type=jnp.float32)
    returning = []
    for scan in range(scans):
        for copy in outgoing[scan]:
            copy.wait()
        for r in range(share):
            block = jnp.concatenate([got_ref[scan, o, r] for o in range(n)], axis=0)
            back = dot32(gram, block)
            for o in range(n):
                back_ref[scan, o, r] = back[o * dets : (o + 1) * dets]
        sent = []
        for o in offsets:
            copy = remote(back_ref.at[scan, o], p_ref.at[scan, pl.ds(me * share, share)],
                          back_sems.at[0, scan, o], back_sems.at[1, scan, o], {"det": behind[o]})
            copy.start()
            sent.append(copy)
        returning.append(sent)
        p_ref[scan, pl.ds(me * share, share)] = back_ref[scan, 0]
    for scan in range(scans):
        for copy in returning[scan]:
            copy.wait()
        streams(scan, w_ref, p_ref, nw_ref, mat_ref, rows_ref, work_ref, out_ref)


def turn_polynomials():
    x = (np.cos(np.pi * (np.arange(400) + 0.5) / 400) + 1) / 8
    t = np.sqrt(x)
    cheb = np.polynomial.Polynomial
    cos_fit = cheb.fit(x, np.cos(2 * np.pi * t), 7).convert().coef
    sin_fit = cheb.fit(x, np.sin(2 * np.pi * t) / t, 7).convert().coef
    return [float(np.float32(c)) for c in cos_fit], [float(np.float32(c)) for c in sin_fit]


COS_FIT, SIN_FIT = turn_polynomials()


def horner(coefficients, x):
    total = jnp.full_like(x, coefficients[-1])
    for c in coefficients[-2::-1]:
        total = total * x + c
    return total


def bin_kernel(gshare, stream_ref, angle_ref, pix_ref, tile_ref, slots_ref, out_ref, target_ref, count_ref):
    strips, dets, _ = stream_ref.shape
    n_slots = slots_ref.shape[1]
    peers = out_ref.shape[0] // CAPD

    def clear(i, carry):
        out_ref[i, :TILE_ROWS, :] = jnp.zeros((TILE_ROWS, LANES), jnp.float32)
        out_ref[i, TILE_ROWS:, :] = jnp.full((8, LANES), -1.0, jnp.float32)
        return carry

    lax.fori_loop(0, peers * CAPD, clear, 0)

    def reset(i, carry):
        count_ref[i] = 0
        return carry

    lax.fori_loop(0, peers, reset, 0)

    def place(i, carry):
        entry = slots_ref[0, i]
        peer = entry // gshare
        rank = count_ref[peer]
        count_ref[peer] = rank + 1
        target = peer * CAPD + rank
        target_ref[i] = target
        out_ref[target, TILE_ROWS:, :] = jnp.full((8, LANES), (entry - peer * gshare).astype(jnp.float32))
        return carry

    lax.fori_loop(0, n_slots, place, 0)

    low_iota = lax.broadcasted_iota(jnp.int32, (LANES, LANES), 0).astype(jnp.float32).astype(jnp.bfloat16)
    high_iota = lax.broadcasted_iota(jnp.int32, (PIX_ROWS, LANES), 0).astype(jnp.float32).astype(jnp.bfloat16)
    one, zero = jnp.bfloat16(1.0), jnp.bfloat16(0.0)

    def strip(s, carry):
        lanes = pl.ds(pl.multiple_of(s * LANES, LANES), LANES)
        value = stream_ref[s]
        turn = angle_ref[0, :, lanes] * (1.0 / math.pi)
        turn = turn - jnp.round(turn)
        square = turn * turn
        parts = [value, value * horner(COS_FIT, square), value * turn * horner(SIN_FIT, square)]
        halves = [split_bf16(v) for v in parts]
        halves = [h[0] for h in halves] + [h[1] for h in halves]
        pix = pix_ref[0, :, lanes]
        high = (pix >> 7).astype(jnp.float32).astype(jnp.bfloat16)
        low = (pix & (LANES - 1)).astype(jnp.float32).astype(jnp.bfloat16)
        for d in range(dets):
            hit = high_iota == high[d : d + 1, :]
            rows = jnp.concatenate([jnp.where(hit, h[d : d + 1, :], zero) for h in halves], axis=0)
            spread = jnp.where(low_iota == low[d : d + 1, :], one, zero)
            both = lax.dot_general(rows, spread, (((1,), (1,)), ((), ())), preferred_element_type=jnp.float32)
            target = target_ref[tile_ref[0, d, s]]
            out_ref[target, :TILE_ROWS, :] += both[:TILE_ROWS] + both[TILE_ROWS:]
        return carry

    lax.fori_loop(0, strips, strip, 0)


def gather_kernel(n, n_tm, tiles_ref, home_ref, out_ref, got_ref, block_ref, homes_ref, owned_ref, det_sems, tm_sems):
    me, me_tm = lax.axis_index("det"), lax.axis_index("tm")
    gshare = home_ref.shape[1]
    barrier = pltpu.get_barrier_semaphore()
    for o in range(1, n):
        pl.semaphore_signal(barrier, inc=1, device_id={"det": lax.rem(me + o, n)}, device_id_type=pl.DeviceIdType.MESH)
    for o in range(1, n_tm):
        pl.semaphore_signal(barrier, inc=1, device_id={"tm": lax.rem(me_tm + o, n_tm)}, device_id_type=pl.DeviceIdType.MESH)
    pl.semaphore_wait(barrier, n + n_tm - 2)
    copies = []
    for o in range(1, n):
        peer = lax.rem(me + o, n)
        copy = remote(tiles_ref.at[pl.ds(peer * CAPD, CAPD)], got_ref.at[o], det_sems.at[0, o], det_sems.at[1, o],
                      {"det": peer})
        copy.start()
        copies.append(copy)
    got_ref[0] = tiles_ref[pl.ds(me * CAPD, CAPD)]
    for o in range(n):
        if o > 0:
            copies[o - 1].wait()
        for e in range(gshare):
            total = None if o == 0 else block_ref[e]
            for i in range(CAPD):
                label = got_ref[o, i, TILE_ROWS : TILE_ROWS + 1, :]
                term = jnp.where(label == float(e), got_ref[o, i, :TILE_ROWS, :], 0.0)
                total = term if total is None else total + term
            block_ref[e] = total
    codes = [jnp.full((1, LANES), home_ref[0, e], jnp.int32) for e in range(gshare)]
    owners = [code // OWN for code in codes]
    places = [code - owner * OWN for code, owner in zip(codes, owners)]
    ranks = []
    for e in range(gshare):
        rank = jnp.zeros((1, LANES), jnp.int32)
        for f in range(e):
            rank = rank + jnp.where(owners[f] == owners[e], 1, 0)
        ranks.append(rank)
    for peer in range(n_tm):
        for rank in range(CAPT):
            tile = jnp.zeros((TILE_ROWS, LANES), jnp.float32)
            label = jnp.full((1, LANES), -1, jnp.int32)
            for e in range(gshare):
                hit = jnp.where(owners[e] * CAPT + ranks[e] == peer * CAPT + rank, 1, 0)
                tile = jnp.where(hit == 1, block_ref[e], tile)
                label = jnp.where(hit == 1, places[e], label)
            homes_ref[peer * CAPT + rank, :TILE_ROWS, :] = tile
            homes_ref[peer * CAPT + rank, TILE_ROWS:, :] = jnp.broadcast_to(label.astype(jnp.float32), (8, LANES))
    copies = []
    for o in range(1, n_tm):
        peer = lax.rem(me_tm + o, n_tm)
        copy = remote(homes_ref.at[pl.ds(peer * CAPT, CAPT)], owned_ref.at[o], tm_sems.at[0, o], tm_sems.at[1, o],
                      {"tm": peer})
        copy.start()
        copies.append(copy)
    owned_ref[0] = homes_ref[pl.ds(me_tm * CAPT, CAPT)]
    for copy in copies:
        copy.wait()
    for t in range(OWN):
        for c in range(3):
            total = jnp.zeros((PIX_ROWS, LANES), jnp.float32)
            for o in range(n_tm):
                for i in range(CAPT):
                    label = owned_ref[o, i, TILE_ROWS : TILE_ROWS + 1, :]
                    part = owned_ref[o, i, c * PIX_ROWS : (c + 1) * PIX_ROWS, :]
                    total = total + jnp.where(label == float(t), part, 0.0)
            for h in range(PIX_ROWS):
                out_ref[t, c : c + 1, h * LANES : (h + 1) * LANES] = total[h : h + 1, :]


def per_device(timestream, polar_angle, pixel_index, strip_tile, time_const, knee_freq, noise_slope,
               white_weight, mode_mix, coupling, device_slots, slot_home):
    dets, total = timestream.shape[1:]
    scans = total // SAMPLES
    n_det, n_tm = lax.axis_size("det"), lax.axis_size("tm")
    matrices, rows = transform_tables()
    matrices, rows = jnp.asarray(matrices), jnp.asarray(rows)
    blocks = 2 * HALF
    share = blocks // n_det
    f32 = jnp.float32
    vmem = pl.BlockSpec(memory_space=pltpu.VMEM)
    smem = pl.BlockSpec(memory_space=pltpu.SMEM)
    stream = pl.pallas_call(
        functools.partial(clean_kernel, n_det),
        out_shape=jax.ShapeDtypeStruct((scans * OUTER, dets, LANES), f32),
        in_specs=[vmem] * 9,
        out_specs=vmem,
        scratch_shapes=[
            pltpu.VMEM((scans, blocks, dets, LANES), f32),
            pltpu.VMEM((scans, blocks, dets, LANES), f32),
            pltpu.VMEM((HALF + 1, dets, LANES), f32),
            pltpu.VMEM((HALF + 1, dets, LANES), f32),
            pltpu.VMEM((HALF * dets, 2 * LANES), f32),
            pltpu.VMEM((dets, LANES), f32),
            pltpu.VMEM((n_det, dets, LANES), f32),
            pltpu.VMEM((scans, n_det, share, dets, LANES), f32),
            pltpu.VMEM((scans, n_det, share, dets, LANES), f32),
            pltpu.SemaphoreType.DMA((2, n_det)),
            pltpu.SemaphoreType.DMA((2, scans, n_det)),
            pltpu.SemaphoreType.DMA((2, scans, n_det)),
        ],
        compiler_params=pltpu.CompilerParams(vmem_limit_bytes=VMEM_LIMIT, collective_id=1, has_side_effects=True),
        name="clean",
    )(timestream, time_const, knee_freq, noise_slope, white_weight, mode_mix, coupling, matrices, rows)
    tiles = pl.pallas_call(
        functools.partial(bin_kernel, slot_home.shape[1]),
        out_shape=jax.ShapeDtypeStruct((n_det * CAPD, SLOT_ROWS, LANES), f32),
        in_specs=[vmem] * 3 + [smem] * 2,
        out_specs=vmem,
        scratch_shapes=[pltpu.SMEM((device_slots.shape[1],), jnp.int32), pltpu.SMEM((n_det,), jnp.int32)],
        compiler_params=pltpu.CompilerParams(vmem_limit_bytes=VMEM_LIMIT),
        name="binning",
    )(stream, polar_angle, pixel_index, strip_tile, device_slots)
    return pl.pallas_call(
        functools.partial(gather_kernel, n_det, n_tm),
        out_shape=jax.ShapeDtypeStruct((OWN, 3, TILE_PIX), f32),
        in_specs=[vmem, smem],
        out_specs=vmem,
        scratch_shapes=[
            pltpu.VMEM((n_det, CAPD, SLOT_ROWS, LANES), f32),
            pltpu.VMEM((slot_home.shape[1], TILE_ROWS, LANES), f32),
            pltpu.VMEM((n_tm * CAPT, SLOT_ROWS, LANES), f32),
            pltpu.VMEM((n_tm, CAPT, SLOT_ROWS, LANES), f32),
            pltpu.SemaphoreType.DMA((2, n_det)),
            pltpu.SemaphoreType.DMA((2, n_tm)),
        ],
        compiler_params=pltpu.CompilerParams(vmem_limit_bytes=VMEM_LIMIT, collective_id=2, has_side_effects=True),
        name="gather",
    )(tiles, slot_home)


def solution(mesh):
    placed = (
        P("tm", "det", None),
        P("tm", "det", None),
        P("tm", "det", None),
        P("tm", "det", None),
        P("tm", "det"),
        P("tm", "det"),
        P("tm", "det"),
        P("tm", "det"),
        P("tm", "det", None),
        P(),
        P("tm", "det"),
        P("tm", "det"),
    )
    return jax.shard_map(
        per_device,
        mesh=mesh,
        in_specs=placed,
        out_specs=P(("tm", "det"), None, None),
        check_vma=False,
    )
```

time: 120 us -> 90.7 us (0.76)
  blocking collectives: 70.4 us -> 0 us
  Pallas kernels: 47 us -> 88.4 us
    all_to_all x4 -> x0, blocking collectives: 70.4 us -> none  [the longest x1 23.2 us: per_device(): got = lax.all_to_all(send, 'det', split_axis=0, concat_axis=0, tiled=True)]
    pallas_call x5 -> x2, Pallas kernels: 13.2 us -> 54.6 us  [the longest x1 36.5 us: per_device(): pl.pallas_call(functools.partial(clean_kernel, n_det), out_shape=jax.Shap...]
where the time goes in v2:
time: 90.7 us; the launch traced here: 90.1 us
  Pallas kernels  88.4 us (97%)
  local copies, waits for them, and re-layouts  1.75 us (2%)
    pallas_call x1, Pallas kernels, per_device(): pl.pallas_call(functools.partial(clean_kernel, n_det), out_shape=jax.Shap...  36.5 us
    pallas_call x1, Pallas kernels, per_device(): pl.pallas_call(functools.partial(bin_kernel, slot_home.shape[1]), out_sha...  33.8 us
    pallas_call x1, Pallas kernels, per_device(): pl.pallas_call(functools.partial(gather_kernel, n_det, n_tm), out_shape=j...  18.1 us

profile of v2, /device:TPU:0, one launch (start us, length us, event | category | flops | bytes accessed | tf_op | source)
XLA Modules:
  0.0 90.1 jit_solution(11698000772105237668)
XLA Ops:
  0.0 36.5 %clean.1.stream_ref = f32[64,16,128]{2,1,0:T(8,128)} custom-call(f32[1,16,8192]{2,1,0:T(8,128)} %ts_ref.1, f32[1,16]{1,0:T(1,128)} %tc_ref.1, f32[1,16]{1,0:T(1,128)} %knee_ref.1, f32[1,16]{1,0:T(1,128)} %slope_ref.1, f32[1,16]{1,0:T(1,128)} %white_ref.1, f32[1,16,64]{2,1,0:T(8,128)} %mix_ref.1, f32[64,64]{1,0:T(8,128)} %cpl_ref.1, ...), custom_call_target="tpu_custom_call" | custom-call | tf_op jit(solution)/shard_map/clean/pallas_call | solution.py:464
  36.6 33.8 %binning.1.tiles_ref = f32[16,56,128]{2,1,0:T(8,128)} custom-call(f32[64,16,128]{2,1,0:T(8,128)} %clean.1.stream_ref, f32[1,16,8192]{2,1,0:T(8,128)} %angle_ref.1, s32[1,16,8192]{2,1,0:T(8,128)} %pix_ref.1, s32[1,16,64]{2,1,0:T(8,128)} %tile_ref.1, s32[1,8]{1,0:T(1,128)} %slots_ref.1), custom_call_target="tpu_custom_call" | custom-call | tf_op jit(solution)/shard_map/binning/pallas_call | solution.py:486
  70.3 18.1 %gather.1 = f32[8,3,2048]{2,1,0:T(4,128)} custom-call(f32[16,56,128]{2,1,0:T(8,128)} %binning.1.tiles_ref, s32[1,4]{1,0:T(1,128)} %home_ref.1), custom_call_target="tpu_custom_call" | custom-call | tf_op jit(solution)/shard_map/gather/pallas_call | solution.py:495
  88.4 1.7 %copy.15 = f32[8,3,2048]{2,0,1:T(8,128)} copy(f32[8,3,2048]{2,1,0:T(4,128)} %gather.1) | data formatting | bytes 393216 | tf_op jit(solution)/shard_map/gather/pallas_call | solution.py:495

commit v3 on v2

--- a/solution.py
+++ b/solution.py
@@ -205,7 +205,7 @@
             w_ref[scan, HALF + k1] = nw_ref[k1] * (im + lag_ref[k1] * re)
 
 
-def streams(scan, w_ref, p_ref, nw_ref, mat_ref, rows_ref, work_ref, out_ref):
+def streams(scan, w_ref, p_ref, nw_ref, mat_ref, rows_ref, work_ref, turns_ref, out_ref):
     dets = w_ref.shape[2]
     for part in range(2):
         for k1 in range(HALF):
@@ -232,7 +232,38 @@
         re.append(last)
         im.append(None)
         for a, value in enumerate(real_backward(re, im)):
-            out_ref[scan * OUTER + a, d0 : d0 + 8, :] = value
+            s = scan * OUTER + a
+            out_ref[s, 0, d0 : d0 + 8, :] = value
+            out_ref[s, 1, d0 : d0 + 8, :] = value * turns_ref[s, 0, d0 : d0 + 8, :]
+            out_ref[s, 2, d0 : d0 + 8, :] = value * turns_ref[s, 1, d0 : d0 + 8, :]
+
+
+def turn_polynomials():
+    x = (np.cos(np.pi * (np.arange(400) + 0.5) / 400) + 1) / 8
+    t = np.sqrt(x)
+    cheb = np.polynomial.Polynomial
+    cos_fit = cheb.fit(x, np.cos(2 * np.pi * t), 7).convert().coef
+    sin_fit = cheb.fit(x, np.sin(2 * np.pi * t) / t, 7).convert().coef
+    return [float(np.float32(c)) for c in cos_fit], [float(np.float32(c)) for c in sin_fit]
+
+
+COS_FIT, SIN_FIT = turn_polynomials()
+
+
+def horner(coefficients, x):
+    total = jnp.full_like(x, coefficients[-1])
+    for c in coefficients[-2::-1]:
+        total = total * x + c
+    return total
+
+
+def turn_angles(scan, angle_ref, turns_ref):
+    for a in range(scan * OUTER, (scan + 1) * OUTER):
+        turn = angle_ref[0, :, a * LANES : (a + 1) * LANES] * (1.0 / math.pi)
+        turn = turn - jnp.round(turn)
+        square = turn * turn
+        turns_ref[a, 0] = horner(COS_FIT, square)
+        turns_ref[a, 1] = turn * horner(SIN_FIT, square)
 
 
 def remote(src, dst, send_sem, recv_sem, device):
@@ -242,8 +273,8 @@
     )
 
 
-def clean_kernel(n, ts_ref, tc_ref, knee_ref, slope_ref, white_ref, mix_ref, cpl_ref, mat_ref, rows_ref, out_ref,
-                 w_ref, p_ref, nw_ref, lag_ref, work_ref, mine_ref, mix_all_ref, got_ref, back_ref,
+def clean_kernel(n, ts_ref, angle_ref, tc_ref, knee_ref, slope_ref, white_ref, mix_ref, cpl_ref, mat_ref, rows_ref, out_ref,
+                 w_ref, p_ref, nw_ref, lag_ref, work_ref, turns_ref, mine_ref, mix_all_ref, got_ref, back_ref,
                  mix_sems, out_sems, back_sems):
     me = lax.axis_index("det")
     scans, rows_all, dets, _ = w_ref.shape
@@ -283,6 +314,7 @@
                            preferred_element_type=jnp.float32)
     returning = []
     for scan in range(scans):
+        turn_angles(scan, angle_ref, turns_ref)
         for copy in outgoing[scan]:
             copy.wait()
         for r in range(share):
@@ -301,30 +333,11 @@
     for scan in range(scans):
         for copy in returning[scan]:
             copy.wait()
-        streams(scan, w_ref, p_ref, nw_ref, mat_ref, rows_ref, work_ref, out_ref)
-
-
-def turn_polynomials():
-    x = (np.cos(np.pi * (np.arange(400) + 0.5) / 400) + 1) / 8
-    t = np.sqrt(x)
-    cheb = np.polynomial.Polynomial
-    cos_fit = cheb.fit(x, np.cos(2 * np.pi * t), 7).convert().coef
-    sin_fit = cheb.fit(x, np.sin(2 * np.pi * t) / t, 7).convert().coef
-    return [float(np.float32(c)) for c in cos_fit], [float(np.float32(c)) for c in sin_fit]
-
-
-COS_FIT, SIN_FIT = turn_polynomials()
-
-
-def horner(coefficients, x):
-    total = jnp.full_like(x, coefficients[-1])
-    for c in coefficients[-2::-1]:
-        total = total * x + c
-    return total
-
-
-def bin_kernel(gshare, stream_ref, angle_ref, pix_ref, tile_ref, slots_ref, out_ref, target_ref, count_ref):
-    strips, dets, _ = stream_ref.shape
+        streams(scan, w_ref, p_ref, nw_ref, mat_ref, rows_ref, work_ref, turns_ref, out_ref)
+
+
+def bin_kernel(gshare, stream_ref, pix_ref, tile_ref, slots_ref, out_ref, rows_ref, target_ref, count_ref):
+    strips, _, dets, _ = stream_ref.shape
     n_slots = slots_ref.shape[1]
     peers = out_ref.shape[0] // CAPD
 
@@ -356,32 +369,48 @@
     low_iota = lax.broadcasted_iota(jnp.int32, (LANES, LANES), 0).astype(jnp.float32).astype(jnp.bfloat16)
     high_iota = lax.broadcasted_iota(jnp.int32, (PIX_ROWS, LANES), 0).astype(jnp.float32).astype(jnp.bfloat16)
     one, zero = jnp.bfloat16(1.0), jnp.bfloat16(0.0)
+    blank = jnp.zeros((LANES, LANES), jnp.bfloat16)
+
+    def prepare(s, carry):
+        lanes = pl.ds(pl.multiple_of(s * LANES, LANES), LANES)
+        for c in range(3):
+            value = stream_ref[s, c]
+            high = value.astype(jnp.bfloat16).astype(jnp.float32)
+            rows_ref[s, c] = high
+            rows_ref[s, 3 + c] = value - high
+        pix = pix_ref[0, :, lanes]
+        rows_ref[s, 6] = (pix >> 7).astype(jnp.float32)
+        rows_ref[s, 7] = (pix & (LANES - 1)).astype(jnp.float32)
+        return carry
+
+    lax.fori_loop(0, strips, prepare, 0, unroll=4)
+
+    def wide(s, i, d):
+        return jnp.broadcast_to(rows_ref[s, i, d : d + 1, :], (16, LANES)).astype(jnp.bfloat16)
 
     def strip(s, carry):
-        lanes = pl.ds(pl.multiple_of(s * LANES, LANES), LANES)
-        value = stream_ref[s]
-        turn = angle_ref[0, :, lanes] * (1.0 / math.pi)
-        turn = turn - jnp.round(turn)
-        square = turn * turn
-        parts = [value, value * horner(COS_FIT, square), value * turn * horner(SIN_FIT, square)]
-        halves = [split_bf16(v) for v in parts]
-        halves = [h[0] for h in halves] + [h[1] for h in halves]
-        pix = pix_ref[0, :, lanes]
-        high = (pix >> 7).astype(jnp.float32).astype(jnp.bfloat16)
-        low = (pix & (LANES - 1)).astype(jnp.float32).astype(jnp.bfloat16)
-        for d in range(dets):
-            hit = high_iota == high[d : d + 1, :]
-            rows = jnp.concatenate([jnp.where(hit, h[d : d + 1, :], zero) for h in halves], axis=0)
-            spread = jnp.where(low_iota == low[d : d + 1, :], one, zero)
-            both = lax.dot_general(rows, spread, (((1,), (1,)), ((), ())), preferred_element_type=jnp.float32)
-            target = target_ref[tile_ref[0, d, s]]
-            out_ref[target, :TILE_ROWS, :] += both[:TILE_ROWS] + both[TILE_ROWS:]
+        for d0 in range(0, dets, 2):
+            rows, spreads = [], []
+            for d in (d0, d0 + 1):
+                hit = high_iota == wide(s, 6, d)
+                rows.append(jnp.concatenate([jnp.where(hit, wide(s, i, d), zero) for i in range(6)], axis=0))
+                low = wide(s, 7, d)
+                spreads.append(jnp.concatenate(
+                    [jnp.where(low_iota[r : r + 16] == low, one, zero) for r in range(0, LANES, 16)], axis=0))
+            spread = jnp.concatenate([
+                jnp.concatenate([spreads[0], blank], axis=1), jnp.concatenate([blank, spreads[1]], axis=1)], axis=0)
+            both = lax.dot_general(jnp.concatenate(rows, axis=1), spread, (((1,), (1,)), ((), ())),
+                                   preferred_element_type=jnp.float32)
+            both = both[:TILE_ROWS] + both[TILE_ROWS:]
+            for d in (d0, d0 + 1):
+                target = target_ref[tile_ref[0, d, s]]
+                out_ref[target, :TILE_ROWS, :] += both[:, (d - d0) * LANES : (d - d0 + 1) * LANES]
         return carry
 
     lax.fori_loop(0, strips, strip, 0)
 
 
-def gather_kernel(n, n_tm, tiles_ref, home_ref, out_ref, got_ref, block_ref, homes_ref, owned_ref, det_sems, tm_sems):
+def gather_kernel(n, n_tm, tiles_ref, home_ref, owned_ref, got_ref, block_ref, homes_ref, det_sems, tm_sems):
     me, me_tm = lax.axis_index("det"), lax.axis_index("tm")
     gshare = home_ref.shape[1]
     barrier = pltpu.get_barrier_semaphore()
@@ -437,6 +466,10 @@
     owned_ref[0] = homes_ref[pl.ds(me_tm * CAPT, CAPT)]
     for copy in copies:
         copy.wait()
+
+
+def place_kernel(owned_ref, out_ref):
+    n_tm = owned_ref.shape[0]
     for t in range(OWN):
         for c in range(3):
             total = jnp.zeros((PIX_ROWS, LANES), jnp.float32)
@@ -446,7 +479,7 @@
                     part = owned_ref[o, i, c * PIX_ROWS : (c + 1) * PIX_ROWS, :]
                     total = total + jnp.where(label == float(t), part, 0.0)
             for h in range(PIX_ROWS):
-                out_ref[t, c : c + 1, h * LANES : (h + 1) * LANES] = total[h : h + 1, :]
+                out_ref[c, t : t + 1, h * LANES : (h + 1) * LANES] = total[h : h + 1, :]
 
 
 def per_device(timestream, polar_angle, pixel_index, strip_tile, time_const, knee_freq, noise_slope,
@@ -463,8 +496,8 @@
     smem = pl.BlockSpec(memory_space=pltpu.SMEM)
     stream = pl.pallas_call(
         functools.partial(clean_kernel, n_det),
-        out_shape=jax.ShapeDtypeStruct((scans * OUTER, dets, LANES), f32),
-        in_specs=[vmem] * 9,
+        out_shape=jax.ShapeDtypeStruct((scans * OUTER, 3, dets, LANES), f32),
+        in_specs=[vmem] * 10,
         out_specs=vmem,
         scratch_shapes=[
             pltpu.VMEM((scans, blocks, dets, LANES), f32),
@@ -472,6 +505,7 @@
             pltpu.VMEM((HALF + 1, dets, LANES), f32),
             pltpu.VMEM((HALF + 1, dets, LANES), f32),
             pltpu.VMEM((HALF * dets, 2 * LANES), f32),
+            pltpu.VMEM((scans * OUTER, 2, dets, LANES), f32),
             pltpu.VMEM((dets, LANES), f32),
             pltpu.VMEM((n_det, dets, LANES), f32),
             pltpu.VMEM((scans, n_det, share, dets, LANES), f32),
@@ -482,32 +516,40 @@
         ],
         compiler_params=pltpu.CompilerParams(vmem_limit_bytes=VMEM_LIMIT, collective_id=1, has_side_effects=True),
         name="clean",
-    )(timestream, time_const, knee_freq, noise_slope, white_weight, mode_mix, coupling, matrices, rows)
+    )(timestream, polar_angle, time_const, knee_freq, noise_slope, white_weight, mode_mix, coupling, matrices, rows)
     tiles = pl.pallas_call(
         functools.partial(bin_kernel, slot_home.shape[1]),
         out_shape=jax.ShapeDtypeStruct((n_det * CAPD, SLOT_ROWS, LANES), f32),
-        in_specs=[vmem] * 3 + [smem] * 2,
+        in_specs=[vmem] * 2 + [smem] * 2,
         out_specs=vmem,
-        scratch_shapes=[pltpu.SMEM((device_slots.shape[1],), jnp.int32), pltpu.SMEM((n_det,), jnp.int32)],
+        scratch_shapes=[pltpu.VMEM((scans * OUTER, 8, dets, LANES), f32), pltpu.SMEM((device_slots.shape[1],), jnp.int32), pltpu.SMEM((n_det,), jnp.int32)],
         compiler_params=pltpu.CompilerParams(vmem_limit_bytes=VMEM_LIMIT),
         name="binning",
-    )(stream, polar_angle, pixel_index, strip_tile, device_slots)
-    return pl.pallas_call(
+    )(stream, pixel_index, strip_tile, device_slots)
+    owned = pl.pallas_call(
         functools.partial(gather_kernel, n_det, n_tm),
-        out_shape=jax.ShapeDtypeStruct((OWN, 3, TILE_PIX), f32),
+        out_shape=jax.ShapeDtypeStruct((n_tm, CAPT, SLOT_ROWS, LANES), f32),
         in_specs=[vmem, smem],
         out_specs=vmem,
         scratch_shapes=[
             pltpu.VMEM((n_det, CAPD, SLOT_ROWS, LANES), f32),
             pltpu.VMEM((slot_home.shape[1], TILE_ROWS, LANES), f32),
             pltpu.VMEM((n_tm * CAPT, SLOT_ROWS, LANES), f32),
-            pltpu.VMEM((n_tm, CAPT, SLOT_ROWS, LANES), f32),
             pltpu.SemaphoreType.DMA((2, n_det)),
             pltpu.SemaphoreType.DMA((2, n_tm)),
         ],
         compiler_params=pltpu.CompilerParams(vmem_limit_bytes=VMEM_LIMIT, collective_id=2, has_side_effects=True),
         name="gather",
     )(tiles, slot_home)
+    out = pl.pallas_call(
+        place_kernel,
+        out_shape=jax.ShapeDtypeStruct((3, OWN, TILE_PIX), f32),
+        in_specs=[vmem],
+        out_specs=vmem,
+        compiler_params=pltpu.CompilerParams(vmem_limit_bytes=VMEM_LIMIT),
+        name="place",
+    )(owned)
+    return jnp.transpose(out, (1, 0, 2))
 
 
 def solution(mesh):

time: 90.7 us -> 90.7 us (level)
  local copies, waits for them, and re-layouts: 1.75 us -> 0 us
  Pallas kernels: 88.4 us -> 90.1 us
    pallas_call x0 -> x1, Pallas kernels: none -> 1.84 us  [per_device(): pl.pallas_call(place_kernel, out_shape=jax.ShapeDtypeStruct((3, OWN, TILE...]
    pallas_call x1 -> x0, local copies, waits for them, and re-layouts: 1.75 us -> none  [per_device(): pl.pallas_call(functools.partial(gather_kernel, n_det, n_tm), out_shape=j...]
where the time goes in v3:
time: 90.7 us; the launch traced here: 90.1 us
  Pallas kernels  90.1 us (99%)
    pallas_call x1, Pallas kernels, per_device(): pl.pallas_call(functools.partial(clean_kernel, n_det), out_shape=jax.Shap...  37.2 us
    pallas_call x1, Pallas kernels, per_device(): pl.pallas_call(functools.partial(bin_kernel, slot_home.shape[1]), out_sha...  33.2 us
    pallas_call x1, Pallas kernels, per_device(): pl.pallas_call(functools.partial(gather_kernel, n_det, n_tm), out_shape=j...  17.9 us
    pallas_call x1, Pallas kernels, per_device(): pl.pallas_call(place_kernel, out_shape=jax.ShapeDtypeStruct((3, OWN, TILE...  1.84 us

profile of v3, /device:TPU:0, one launch (start us, length us, event | category | flops | bytes accessed | tf_op | source)
XLA Modules:
  0.0 90.1 jit_solution(12508811056654719355)
XLA Ops:
  0.0 37.2 %clean.1.stream_ref = f32[64,3,16,128]{3,2,1,0:T(8,128)} custom-call(f32[1,16,8192]{2,1,0:T(8,128)} %ts_ref.1, f32[1,16,8192]{2,1,0:T(8,128)} %angle_ref.1, f32[1,16]{1,0:T(1,128)} %tc_ref.1, f32[1,16]{1,0:T(1,128)} %knee_ref.1, f32[1,16]{1,0:T(1,128)} %slope_ref.1, f32[1,16]{1,0:T(1,128)} %white_ref.1, f32[1,16,64]{2,1,0:T(8,128)} %mix_ref.1, ...), custom_call_target="tpu_custom_call" | custom-call | tf_op jit(solution)/shard_map/clean/pallas_call | solution.py:497
  37.2 33.2 %binning.1.tiles_ref = f32[16,56,128]{2,1,0:T(8,128)} custom-call(f32[64,3,16,128]{3,2,1,0:T(8,128)} %clean.1.stream_ref, s32[1,16,8192]{2,1,0:T(8,128)} %pix_ref.1, s32[1,16,64]{2,1,0:T(8,128)} %tile_ref.1, s32[1,8]{1,0:T(1,128)} %slots_ref.1), custom_call_target="tpu_custom_call" | custom-call | tf_op jit(solution)/shard_map/binning/pallas_call | solution.py:520
  70.4 17.9 %gather.1.owned_ref = f32[4,2,56,128]{3,2,1,0:T(8,128)} custom-call(f32[16,56,128]{2,1,0:T(8,128)} %binning.1.tiles_ref, s32[1,4]{1,0:T(1,128)} %home_ref.1), custom_call_target="tpu_custom_call" | custom-call | tf_op jit(solution)/shard_map/gather/pallas_call | solution.py:529
  88.3 1.8 %place.1 = f32[3,8,2048]{2,1,0:T(8,128)} custom-call(f32[4,2,56,128]{3,2,1,0:T(8,128)} %gather.1.owned_ref), custom_call_target="tpu_custom_call" | custom-call | tf_op jit(solution)/shard_map/place/pallas_call | solution.py:544

commit v4 on v3

--- a/solution.py
+++ b/solution.py
@@ -366,9 +366,9 @@
 
     lax.fori_loop(0, n_slots, place, 0)
 
-    low_iota = lax.broadcasted_iota(jnp.int32, (LANES, LANES), 0).astype(jnp.float32).astype(jnp.bfloat16)
+    low_iota = lax.broadcasted_iota(jnp.int32, (LANES, LANES), 1).astype(jnp.float32)
     high_iota = lax.broadcasted_iota(jnp.int32, (PIX_ROWS, LANES), 0).astype(jnp.float32).astype(jnp.bfloat16)
-    one, zero = jnp.bfloat16(1.0), jnp.bfloat16(0.0)
+    zero = jnp.bfloat16(0.0)
     blank = jnp.zeros((LANES, LANES), jnp.bfloat16)
 
     def prepare(s, carry):
@@ -389,17 +389,17 @@
         return jnp.broadcast_to(rows_ref[s, i, d : d + 1, :], (16, LANES)).astype(jnp.bfloat16)
 
     def strip(s, carry):
+        lows = jnp.transpose(rows_ref[s, 7])
         for d0 in range(0, dets, 2):
             rows, spreads = [], []
             for d in (d0, d0 + 1):
                 hit = high_iota == wide(s, 6, d)
                 rows.append(jnp.concatenate([jnp.where(hit, wide(s, i, d), zero) for i in range(6)], axis=0))
-                low = wide(s, 7, d)
-                spreads.append(jnp.concatenate(
-                    [jnp.where(low_iota[r : r + 16] == low, one, zero) for r in range(0, LANES, 16)], axis=0))
+                low = jnp.broadcast_to(lows[:, d : d + 1], (LANES, LANES))
+                spreads.append(jnp.where(low_iota == low, 1.0, 0.0).astype(jnp.bfloat16))
             spread = jnp.concatenate([
                 jnp.concatenate([spreads[0], blank], axis=1), jnp.concatenate([blank, spreads[1]], axis=1)], axis=0)
-            both = lax.dot_general(jnp.concatenate(rows, axis=1), spread, (((1,), (1,)), ((), ())),
+            both = lax.dot_general(jnp.concatenate(rows, axis=1), spread, (((1,), (0,)), ((), ())),
                                    preferred_element_type=jnp.float32)
             both = both[:TILE_ROWS] + both[TILE_ROWS:]
             for d in (d0, d0 + 1):

time: 90.7 us -> 104 us (1.15)
  Pallas kernels: 90.1 us -> 103 us
    pallas_call x1, Pallas kernels: 33.2 us -> 46.6 us  [per_device(): pl.pallas_call(functools.partial(bin_kernel, slot_home.shape[1]), out_sha...]
where the time goes in v4:
time: 104 us; the launch traced here: 103 us
  Pallas kernels  103 us (99%)
    pallas_call x1, Pallas kernels, per_device(): pl.pallas_call(functools.partial(bin_kernel, slot_home.shape[1]), out_sha...  46.6 us
    pallas_call x1, Pallas kernels, per_device(): pl.pallas_call(functools.partial(clean_kernel, n_det), out_shape=jax.Shap...  37.2 us
    pallas_call x1, Pallas kernels, per_device(): pl.pallas_call(functools.partial(gather_kernel, n_det, n_tm), out_shape=j...  17.8 us

profile of v4, /device:TPU:0, one launch (start us, length us, event | category | flops | bytes accessed | tf_op | source)
XLA Modules:
  0.0 103.4 jit_solution(13269422238003877344)
XLA Ops:
  0.0 37.2 %clean.1.stream_ref = f32[64,3,16,128]{3,2,1,0:T(8,128)} custom-call(f32[1,16,8192]{2,1,0:T(8,128)} %ts_ref.1, f32[1,16,8192]{2,1,0:T(8,128)} %angle_ref.1, f32[1,16]{1,0:T(1,128)} %tc_ref.1, f32[1,16]{1,0:T(1,128)} %knee_ref.1, f32[1,16]{1,0:T(1,128)} %slope_ref.1, f32[1,16]{1,0:T(1,128)} %white_ref.1, f32[1,16,64]{2,1,0:T(8,128)} %mix_ref.1, ...), custom_call_target="tpu_custom_call" | custom-call | tf_op jit(solution)/shard_map/clean/pallas_call | solution.py:497
  37.2 46.6 %binning.1.tiles_ref = f32[16,56,128]{2,1,0:T(8,128)} custom-call(f32[64,3,16,128]{3,2,1,0:T(8,128)} %clean.1.stream_ref, s32[1,16,8192]{2,1,0:T(8,128)} %pix_ref.1, s32[1,16,64]{2,1,0:T(8,128)} %tile_ref.1, s32[1,8]{1,0:T(1,128)} %slots_ref.1), custom_call_target="tpu_custom_call" | custom-call | tf_op jit(solution)/shard_map/binning/pallas_call | solution.py:520
  83.7 17.8 %gather.1.owned_ref = f32[4,2,56,128]{3,2,1,0:T(8,128)} custom-call(f32[16,56,128]{2,1,0:T(8,128)} %binning.1.tiles_ref, s32[1,4]{1,0:T(1,128)} %home_ref.1), custom_call_target="tpu_custom_call" | custom-call | tf_op jit(solution)/shard_map/gather/pallas_call | solution.py:529
  101.6 1.8 %place.1 = f32[3,8,2048]{2,1,0:T(8,128)} custom-call(f32[4,2,56,128]{3,2,1,0:T(8,128)} %gather.1.owned_ref), custom_call_target="tpu_custom_call" | custom-call | tf_op jit(solution)/shard_map/place/pallas_call | solution.py:544
